TPU v7x, 128 devices: a whole 4x4x4 slice. The times are simulated.
128 devices in a mesh: ctx: 32 (over x, y, core), section: 4 (over z).
Axes of the slice: x: 4, y: 4, z: 4, core: 2. Of those that a mesh axis runs over, the one named last changes fastest.
Arguments:
- query_rows: bfloat16 [65536, 1024], P(('ctx', 'section')), may hold values from -5 to 5
- key_rows: bfloat16 [65536, 128], P(('ctx', 'section')), may hold values from -5 to 5
- value_rows: bfloat16 [65536, 128], P(('ctx', 'section')), may hold values from -5 to 5
- attn_out: bfloat16 [65536, 1024], P(('ctx', 'section')), may hold values from -2 to 2
- out_grad: bfloat16 [65536, 1024], P(('ctx', 'section')), may hold values from -5 to 5
- log_total: float32 [8, 65536], P(None, ('ctx', 'section')), may hold values from -300 to 300
- doc_lengths: int32 [128], replicated, may hold values from 1 to 4096, as said below
Outputs:
- query_grad: bfloat16 [65536, 1024], P(('ctx', 'section'))
- key_grad: bfloat16 [65536, 128], P(('ctx', 'section'))
- value_grad: bfloat16 [65536, 128], P(('ctx', 'section'))
Inputs may be any that keep to these rules, and one draw needn't show every extreme that they name: `doc_lengths`: the documents fill all 65536 positions; the longest has exactly 4096 tokens.
All inputs are finite; a program needn't handle non-finite values.
Results may differ from a plain program's by a relative error of at most 0.005.
Values may be sent and summed in bfloat16 or wider, within the bound.
A program may use at most 64 MiB of HBM per device.

v0:
```python
import functools
import math

import jax
import jax.numpy as jnp
from jax import lax
from jax.experimental import pallas as pl
from jax.experimental.pallas import tpu as pltpu
from jax.sharding import PartitionSpec as P

MESH = pl.DeviceIdType.MESH
W = 128
B = 256
VMEM = 58 << 20
LOG2E = math.log2(math.e)
OWN, BEFORE = 1, 0


def nn(a, b):
    return jnp.dot(a, b, preferred_element_type=jnp.float32)


def nt(a, b):
    return lax.dot_general(a, b, (((1,), (1,)), ((), ())), preferred_element_type=jnp.float32)


def place():
    ctx = lax.axis_index("ctx")
    return ctx // 2, lax.axis_index("section"), ctx % 2


def slot(side, z, j):
    return side * 8 + z * 2 + j


def doc_ends(docs_ref):
    lengths = docs_ref[...].astype(jnp.float32)
    docs = lengths.shape[1]
    upto = lax.broadcasted_iota(jnp.int32, (docs, docs), 1) <= lax.broadcasted_iota(
        jnp.int32, (docs, docs), 0
    )
    return jnp.sum(jnp.where(upto, lengths, 0.0), axis=1, keepdims=True)


def positions(first):
    return first.astype(jnp.float32) + lax.broadcasted_iota(jnp.int32, (1, B), 1).astype(
        jnp.float32
    )


def doc_start(ends, pos):
    return jnp.max(jnp.where(ends <= pos, ends, 0.0), axis=0, keepdims=True)


def hidden(key, start, pos):
    kpos = (key + lax.broadcasted_iota(jnp.int32, (B, B), 0)).astype(jnp.float32)
    return jnp.where((kpos >= start) & (kpos <= pos), 0.0, -jnp.inf)


def identity(n):
    at = [lax.broadcasted_iota(jnp.int32, (n, n), d) for d in range(2)]
    return (at[0] == at[1]).astype(jnp.bfloat16)


def gradients(k, v, qs, gs, logs, deltas, bias=None):
    ps, ds = [], []
    for q, g, log, delta in zip(qs, gs, logs, deltas):
        x = nt(k, q) * (LOG2E / math.sqrt(W)) - log
        if bias is not None:
            x = x + bias[...]
        p = jnp.exp2(x)
        d = p * (nt(v, g) - delta)
        ps.append(p.astype(jnp.bfloat16))
        ds.append(d.astype(jnp.bfloat16))
    dh = jnp.concatenate(ds, axis=1)
    dv = nn(jnp.concatenate(ps, axis=1), jnp.concatenate(gs, axis=0))
    dk = nn(dh, jnp.concatenate(qs, axis=0))
    return dk, dv, nn(k.T, dh)


class Links:
    def __init__(self, columns):
        self.column, self.z, self.core = place()
        ctx = lax.axis_index("ctx")
        self.up = lax.rem(self.z + 1, 4)
        self.down = lax.rem(self.z + 3, 4)
        self.across = lax.rem(self.z + 2, 4)
        self.sibling = (ctx + 1 - 2 * self.core, self.z)
        self.above = (ctx, self.up)
        self.below = (ctx, self.down)
        self.has_next = self.column < columns - 1
        self.has_last = self.column > 0
        self.next = (jnp.where(self.has_next, ctx + 2, ctx), self.z)
        self.last = (jnp.where(self.has_last, ctx - 2, ctx), self.z)
        self.next_across = (self.next[0], self.across)
        self.last_across = (self.last[0], self.across)

    def barrier(self, straight=False):
        barrier = pltpu.get_barrier_semaphore()

        def greet(*devices):
            for device in devices:
                pl.semaphore_signal(barrier, inc=1, device_id=device, device_id_type=MESH)

        greet(self.sibling, self.above, self.below)
        later = (self.next, self.next_across) if straight else (self.next,)
        earlier = (self.last, self.last_across) if straight else (self.last,)
        pl.when(self.has_next)(lambda: greet(*later))
        pl.when(self.has_last)(lambda: greet(*earlier))
        columns = self.has_next.astype(jnp.int32) + self.has_last.astype(jnp.int32)
        pl.semaphore_wait(barrier, 3 + len(later) * columns)


class Route:
    def __init__(self, sems, index, device, source, target, sends=True, gets=True, arrival=None):
        self.sends, self.gets = sends, gets
        landed = target if arrival is None else arrival
        send, recv = sems[0].at[index], sems[1].at[index]
        self.make = lambda end: pltpu.make_async_remote_copy(
            source, end, send, recv, device_id=device, device_id_type=MESH
        )
        self.target, self.landed = target, landed

    @staticmethod
    def only(condition, act):
        if condition is True:
            act()
        else:
            pl.when(condition)(act)

    def start(self):
        self.only(self.sends, lambda: self.make(self.target).start())

    def arrived(self):
        self.only(self.gets, lambda: self.make(self.landed).wait_recv())

    def sent(self):
        self.only(self.sends, lambda: self.make(self.target).wait_send())


def gather_kernel(
    columns, heads, docs_ref, q_ref, g_ref, o_ref, k_ref, v_ref, log_ref,
    q_other, g_other, stat_both, window_out, dq_out, kv_out,
    q_both, g_both, o_vmem, k_own, v_own, stat, window, dqt, dkv, bias, local, put, send, recv,
):
    at = Links(columns)
    z, core, up, down, across = at.z, at.core, at.up, at.down, at.across
    sems = (send, recv)
    mine = window.at[slot(OWN, z, core)]
    loads = [
        pltpu.make_async_copy(source, target, local.at[n])
        for n, (source, target) in enumerate(
            (
                (k_ref, k_own), (v_ref, v_own), (q_ref, q_both.at[0]), (g_ref, g_both.at[0]),
                (o_ref, o_vmem), (log_ref, stat.at[0, 0]),
            )
        )
    ]
    for copy in loads:
        copy.start()

    @pl.when(at.column == 0)
    def _():
        window[slot(BEFORE, 3, 1)] = jnp.zeros((2, B, W), window.dtype)

    at.barrier()

    theirs = window.at[slot(OWN, z, 1 - core)]
    swap_k = Route(sems, 0, at.sibling, k_own.at[B:], mine.at[0], arrival=theirs.at[0])
    swap_v = Route(sems, 1, at.sibling, v_own.at[B:], mine.at[1], arrival=theirs.at[1])
    loads[0].wait()
    loads[1].wait()
    swap_k.start()
    swap_v.start()
    mine[0] = k_own[:B]
    mine[1] = v_own[:B]
    rows = q_ref.shape[0]
    bulk = []
    for part in range(2):
        some = slice(part * rows // 2, (part + 1) * rows // 2)
        bulk.append(Route(sems, 2 + part, at.sibling, q_both.at[0, some], q_both.at[1, some]))
        bulk.append(Route(sems, 4 + part, at.sibling, g_both.at[0, some], g_both.at[1, some]))

    def passed(index, device, side, sent, j, got, sends=True, gets=True):
        there = window.at[slot(side, sent, j)]
        return Route(sems, index, device, there, there, sends, gets, window.at[slot(side, got, j)])

    up_0 = passed(6, at.above, OWN, z, 0, down)
    up_1 = passed(7, at.above, OWN, z, 1, down)
    down_0 = passed(8, at.below, OWN, z, 0, up)
    down_1 = passed(9, at.below, OWN, z, 1, up, z == 0, z == 3)
    far_0 = passed(10, at.below, OWN, up, 0, across)
    far_1 = passed(11, at.above, OWN, down, 1, across)

    def later(index, zc, j, when=True):
        here = window.at[slot(OWN, zc, j)]
        there = window.at[slot(BEFORE, zc, j)]
        sends = at.has_next if when is True else at.has_next & when
        gets = at.has_last if when is True else at.has_last & when
        return Route(sems, index, at.next, here, there, sends, gets)

    next_0 = later(12, z, 0)
    next_1 = later(13, z, 1)
    next_far_0 = later(14, across, 0, z < 2)
    next_far_1 = later(15, across, 1)
    last = at.has_last
    before_up_0 = passed(16, at.above, BEFORE, z, 0, down, last & (z == 3), last & (z == 0))
    before_up_1 = passed(17, at.above, BEFORE, z, 1, down, last, last)
    before_down_0 = passed(18, at.below, BEFORE, z, 0, up, last & (z != 0), last & (z != 3))
    before_down_1 = passed(19, at.below, BEFORE, z, 1, up, last, last)
    stats = Route(sems, 20, at.sibling, stat.at[0], stat.at[1])

    swap_k.arrived()
    swap_v.arrived()
    for copy in (up_1, down_0, next_1):
        copy.start()
    for copy in loads[2:]:
        copy.wait()

    ones = jnp.ones((8, W), jnp.bfloat16)
    for h in range(heads):
        cols = slice(h * W, (h + 1) * W)
        product = g_both[0, :, cols].astype(jnp.float32) * o_vmem[:, cols].astype(jnp.float32)
        high = product.astype(jnp.bfloat16)
        low = (product - high.astype(jnp.float32)).astype(jnp.bfloat16)
        total = nt(ones, high) + nt(ones, low)
        stat[0, 1, h : h + 1, :] = total[0:1]
    stat[0, 0] = stat[0, 0] * LOG2E
    stats.start()
    for copy in (next_0, up_0, down_1):
        copy.start()
    for copy in bulk:
        copy.start()

    ends = doc_ends(docs_ref)
    column = at.column * 16 * B
    dkv[...] = jnp.zeros_like(dkv)
    dqt[...] = jnp.zeros_like(dqt)

    def products(side, part, k, v, mask):
        here = pl.ds(pl.multiple_of(part * B, B), B)
        return gradients(
            k, v,
            [q_both[side, here, h * W : (h + 1) * W] for h in range(heads)],
            [g_both[side, here, h * W : (h + 1) * W] for h in range(heads)],
            [stat[side, 0, h : h + 1, here] for h in range(heads)],
            [stat[side, 1, h : h + 1, here] for h in range(heads)],
            mask,
        )

    up_1.arrived()
    far_1.start()
    down_0.arrived()
    far_0.start()
    next_1.arrived()
    before_down_1.start()
    before_up_1.start()
    next_0.arrived()
    before_down_0.start()
    before_up_0.start()

    near_4 = jnp.where(z > 0, slot(OWN, down, 1), slot(OWN, 3, 0))
    near_0 = jnp.where(z > 0, slot(OWN, down, 0), slot(BEFORE, 3, 1))

    def half_of(tile):
        return jnp.where((tile + 8) % 8 >= 4, 1 - core, core)

    def near(side, part, tile, keys, key_tiles, out):
        start = doc_start(ends, positions(column + tile * 2 * B + part * B))
        for n, key_tile in enumerate(key_tiles):
            key = column + key_tile * 2 * B + half_of(key_tile) * B
            kpos = (key + lax.broadcasted_iota(jnp.int32, (B, B), 0)).astype(jnp.float32)
            bias[n * B : (n + 1) * B] = jnp.where(kpos >= start, 0.0, -jnp.inf)
        dk, dv, dq = products(
            side, part,
            jnp.concatenate([window[n, 0] for n in keys], axis=0),
            jnp.concatenate([window[n, 1] for n in keys], axis=0),
            bias.at[: len(keys) * B],
        )
        for n in range(len(keys)):
            dkv[out + n, 0] += dk[n * B : (n + 1) * B]
            dkv[out + n, 1] += dv[n * B : (n + 1) * B]
        dqt[side * 2 + part] += dq

    puts = [
        pltpu.make_async_copy(source, target, put.at[n])
        for n, (source, target) in enumerate(
            (
                (q_both.at[1], q_other), (g_both.at[1], g_other), (stat, stat_both),
                (window.at[8:], window_out.at[8:]), (dqt.at[:2], dq_out.at[:2]),
                (window.at[:8], window_out.at[:8]), (dqt.at[2:], dq_out.at[2:]), (dkv, kv_out),
            )
        )
    ]

    @pl.loop(0, 4)
    def _(n):
        @pl.when(n == 0)
        def _():
            up_0.arrived()
            pl.when((core == 0) & (z == 0))(before_up_1.arrived)

        @pl.when(n == 1)
        def _():
            far_0.arrived()
            next_far_0.start()
            far_1.arrived()
            next_far_1.start()

        @pl.when(n == 2)
        def _():
            down_1.arrived()
            for copy in bulk:
                copy.arrived()
            stats.arrived()
            pl.when((core == 1) & (z == 0))(before_up_1.arrived)
            for copy in puts[:5]:
                copy.start()

        side, part = n // 2, n % 2

        @pl.when(side == core)
        def _():
            near(side, part, z, [near_0], [z - 1], 2)

        @pl.when(side != core)
        def _():
            near(side, part, z + 4, [slot(OWN, z, 0), near_4], [z, z + 3], 0)

    puts[6].start()
    puts[7].start()
    pl.when(z != 0)(before_up_1.arrived)
    for copy in (before_up_0, before_down_0, before_down_1, next_far_0, next_far_1):
        copy.arrived()
    puts[5].start()
    for copy in (
        [swap_k, swap_v, up_0, up_1, down_0, down_1, far_0, far_1, next_0, next_1, next_far_0]
        + [next_far_1, before_up_0, before_up_1, before_down_0, before_down_1, stats]
        + bulk
    ):
        copy.sent()
    for copy in puts:
        copy.wait()


def gather(columns, docs, q, g, o, k, v, log_total):
    rows, features = q.shape
    heads = features // W
    some = pl.BlockSpec(memory_space=pl.ANY)
    window = (16, 2, B, W)
    stat = (2, 2, heads, rows)
    turned = (4, W, heads * B)
    sums = (3, 2, B, W)
    return pl.pallas_call(
        functools.partial(gather_kernel, columns, heads),
        out_shape=(
            jax.ShapeDtypeStruct(q.shape, q.dtype),
            jax.ShapeDtypeStruct(q.shape, q.dtype),
            jax.ShapeDtypeStruct(stat, jnp.float32),
            jax.ShapeDtypeStruct(window, k.dtype),
            jax.ShapeDtypeStruct(turned, jnp.float32),
            jax.ShapeDtypeStruct(sums, jnp.float32),
        ),
        in_specs=[pl.BlockSpec(memory_space=pltpu.VMEM)] + [some] * 6,
        out_specs=(some,) * 6,
        scratch_shapes=[
            pltpu.VMEM((2, rows, features), q.dtype),
            pltpu.VMEM((2, rows, features), q.dtype),
            pltpu.VMEM(q.shape, q.dtype),
            pltpu.VMEM(k.shape, k.dtype),
            pltpu.VMEM(k.shape, k.dtype),
            pltpu.VMEM(stat, jnp.float32),
            pltpu.VMEM(window, k.dtype),
            pltpu.VMEM(turned, jnp.float32),
            pltpu.VMEM(sums, jnp.float32),
            pltpu.VMEM((2 * B, B), jnp.float32),
            pltpu.SemaphoreType.DMA((6,)),
            pltpu.SemaphoreType.DMA((8,)),
            pltpu.SemaphoreType.DMA((21,)),
            pltpu.SemaphoreType.DMA((21,)),
        ],
        compiler_params=pltpu.CompilerParams(
            collective_id=0, has_side_effects=True, vmem_limit_bytes=VMEM
        ),
    )(docs, q, g, o, k, v, log_total)


def attend_kernel(
    heads, docs_ref, qa_hbm, qb_hbm, ga_hbm, gb_hbm, stat_hbm, window_hbm, dq_hbm, kv_hbm,
    dq_own, dq_other, part_hbm,
    q_ref, g_ref, stat_ref, window_ref, dqt, dqh, part_ref, dka, dva, dkv, bias, starts, bounds, get, put,
):
    column, z, core = place()
    loads = [
        pltpu.make_async_copy(source, target, get.at[n])
        for n, (source, target) in enumerate(
            (
                (stat_hbm, stat_ref),
                (window_hbm.at[:8], window_ref.at[:8]), (window_hbm.at[8:], window_ref.at[8:]),
                (kv_hbm, dkv), (qa_hbm, q_ref.at[0]), (ga_hbm, g_ref.at[0]),
                (dq_hbm.at[:2], dqt.at[:2]),
                (qb_hbm, q_ref.at[1]), (gb_hbm, g_ref.at[1]), (dq_hbm.at[2:], dqt.at[2:]),
            )
        )
    ]
    for load in loads:
        load.start()
    ends = doc_ends(docs_ref)
    window = (column - 1) * 16 * B

    def half_of(b):
        return jnp.where(b % 8 >= 4, 1 - core, core)

    def tile_of(side):
        return z + 4 * (core if side == 0 else 1 - core)

    for block in range(4):
        side, part = divmod(block, 2)
        first = column * 16 * B + tile_of(side) * 2 * B + part * B
        start = doc_start(ends, positions(first))
        starts[block] = start
        low = jnp.min(start).astype(jnp.int32) - window
        last = jnp.max(start).astype(jnp.int32) - window
        b = low // (2 * B)
        bounds[0, block] = jnp.where(low % (2 * B) >= half_of(b) * B + B, b + 1, b)
        b = last // (2 * B)
        bounds[1, block] = jnp.where(last % (2 * B) > half_of(b) * B, b + 1, b)
    dka[...] = jnp.zeros_like(dka)
    dva[...] = jnp.zeros_like(dva)
    for load in loads[:7]:
        load.wait()
    down = lax.rem(z + 3, 4)
    nears = (
        slot(OWN, z, 0),
        jnp.where(z > 0, slot(OWN, down, 1), slot(OWN, 3, 0)),
        jnp.where(z > 0, slot(OWN, down, 0), slot(BEFORE, 3, 1)),
    )
    for n, at in enumerate(nears):
        dka[at] = dkv[n, 0]
        dva[at] = dkv[n, 1]

    @pl.loop(0, 4)
    def _(block):
        side, part = block // 2, block % 2
        here = pl.ds(pl.multiple_of(part * B, B), B)

        @pl.when(block == 2)
        def _():
            for load in loads[7:]:
                load.wait()

        def work(blocks, mask=None):
            at = [slot(b // 8, b % 4, b % 8 // 4) for b in blocks]
            dk, dv, dq = gradients(
                jnp.concatenate([window_ref[n, 0] for n in at], axis=0),
                jnp.concatenate([window_ref[n, 1] for n in at], axis=0),
                [q_ref[side, here, h * W : (h + 1) * W] for h in range(heads)],
                [g_ref[side, here, h * W : (h + 1) * W] for h in range(heads)],
                [stat_ref[side, 0, h : h + 1, here] for h in range(heads)],
                [stat_ref[side, 1, h : h + 1, here] for h in range(heads)],
                mask,
            )
            for n in range(len(at)):
                dva[at[n]] += dv[n * B : (n + 1) * B]
                dka[at[n]] += dk[n * B : (n + 1) * B]
            dqt[block] += dq

        second = jnp.where(side == 0, core, 1 - core)
        end = 7 + z + 4 * second
        skip = jnp.where(second == 1, 8 + z, 16)

        def counted(b):
            return jnp.where(b > skip, b - 1, b)

        def real(n):
            return jnp.where(n >= skip, n + 1, n)

        end = counted(end)
        low = counted(bounds[0, block])
        cut = jnp.minimum(counted(bounds[1, block]), end)
        cut = cut + (end - cut) % 2

        @pl.loop(low, cut)
        def _(n):
            b = real(n)
            key = window + b * 2 * B + half_of(b) * B
            kpos = (key + lax.broadcasted_iota(jnp.int32, (B, B), 0)).astype(jnp.float32)
            bias[...] = jnp.where(kpos >= starts[block], 0.0, -jnp.inf)
            work([b], bias)

        @pl.loop(0, (end - jnp.maximum(low, cut)) // 2)
        def _(n):
            work([real(cut + 2 * n), real(cut + 2 * n + 1)])

        @pl.when(side == 0)
        def _():
            pltpu.make_async_copy(dqt.at[block], dq_own.at[part], put.at[block]).start()

        @pl.when(side == 1)
        def _():
            dqh[part] = dqt[block].astype(jnp.bfloat16)
            pltpu.make_async_copy(dqh.at[part], dq_other.at[part], put.at[block]).start()

    @pl.loop(0, 16)
    def _(s):
        part_ref[s, 0] = (dka[s] * (1.0 / math.sqrt(W))).astype(jnp.bfloat16)
        part_ref[s, 1] = dva[s].astype(jnp.bfloat16)
        pltpu.make_async_copy(part_ref.at[s], part_hbm.at[s], put.at[4 + s]).start()

    for part in range(2):
        pltpu.make_async_copy(dqt.at[part], dq_own.at[part], put.at[part]).wait()
        pltpu.make_async_copy(dqh.at[part], dq_other.at[part], put.at[2 + part]).wait()
    for s in range(16):
        pltpu.make_async_copy(part_ref.at[s], part_hbm.at[s], put.at[4 + s]).wait()


def attend(docs, q, q_other, g, g_other, stat, window, dq, sums):
    rows, features = q.shape
    heads = features // W
    some = pl.BlockSpec(memory_space=pl.ANY)
    both = (2, rows, features)
    turned = (2, W, heads * B)
    return pl.pallas_call(
        functools.partial(attend_kernel, heads),
        out_shape=(
            jax.ShapeDtypeStruct(turned, jnp.float32),
            jax.ShapeDtypeStruct(turned, jnp.bfloat16),
            jax.ShapeDtypeStruct(window.shape, jnp.bfloat16),
        ),
        in_specs=[pl.BlockSpec(memory_space=pltpu.VMEM)] + [some] * 8,
        out_specs=(some,) * 3,
        scratch_shapes=[
            pltpu.VMEM(both, q.dtype),
            pltpu.VMEM(both, q.dtype),
            pltpu.VMEM(stat.shape, stat.dtype),
            pltpu.VMEM(window.shape, window.dtype),
            pltpu.VMEM((4, W, heads * B), jnp.float32),
            pltpu.VMEM(turned, jnp.bfloat16),
            pltpu.VMEM(window.shape, jnp.bfloat16),
            pltpu.VMEM((16, B, W), jnp.float32),
            pltpu.VMEM((16, B, W), jnp.float32),
            pltpu.VMEM(sums.shape, jnp.float32),
            pltpu.VMEM((B, B), jnp.float32),
            pltpu.VMEM((4, 1, B), jnp.float32),
            pltpu.SMEM((2, 4), jnp.int32),
            pltpu.SemaphoreType.DMA((10,)),
            pltpu.SemaphoreType.DMA((20,)),
        ],
        compiler_params=pltpu.CompilerParams(vmem_limit_bytes=VMEM),
        cost_estimate=pl.CostEstimate(
            flops=20 * 10 * heads * B * B * W, bytes_accessed=16 << 20, transcendentals=0
        ),
    )(docs, q, q_other, g, g_other, stat, window, dq, sums)


def return_kernel(
    columns, heads, docs_ref, q_hbm, k_hbm, v_hbm, g_hbm, stat_hbm, dq_own, dq_other, part_ref,
    dq_hbm, dk_hbm, dv_hbm,
    q_ref, k_ref, v_ref, g_ref, stat, dqt, dq_sent, dq_got, dq_out, dk_ref, dv_ref, dka, dva, bias,
    part, across_got, beside_got, beside_sum, later_got, far_got, far_sum, near_sum,
    near_got, final, given_half, local, put, send, recv,
):
    at = Links(columns)
    z, core, up, down, across = at.z, at.core, at.up, at.down, at.across
    sems = (send, recv)
    load = pltpu.make_async_copy(part_ref.at[:8], part.at[:8], local.at[0])
    load_own = pltpu.make_async_copy(part_ref.at[8:], part.at[8:], local.at[1])
    load_dq = pltpu.make_async_copy(dq_other, dq_sent, local.at[2])
    load.start()
    load_own.start()
    load_dq.start()
    loads = [
        pltpu.make_async_copy(source, target, local.at[3 + n])
        for n, (source, target) in enumerate(
            (
                (q_hbm, q_ref), (g_hbm, g_ref), (k_hbm, k_ref), (v_hbm, v_ref),
                (stat_hbm.at[0], stat), (dq_own, dqt),
            )
        )
    ]
    for copy in loads:
        copy.start()
    at.barrier()
    has_next, has_last = at.has_next, at.has_last

    def given(side, zc, j):
        return part.at[slot(side, zc, j)]

    def held(side, zc, j):
        return part[slot(side, zc, j)].astype(jnp.float32)

    far_back = [
        Route(
            sems, j, at.last, given(BEFORE, across, j), across_got.at[j],
            has_last & (z < 2) if j == 0 else has_last,
            has_next & (z < 2) if j == 0 else has_next,
        )
        for j in range(2)
    ]
    side_up = [
        Route(
            sems, 2 + j, at.above, given(BEFORE, up, j), beside_got.at[0, j],
            has_last & (z != 3) if j == 0 else has_last,
            has_last & (z != 0) if j == 0 else has_last,
        )
        for j in range(2)
    ]
    side_down = [
        Route(
            sems, 4 + j, at.below, given(BEFORE, down, j), beside_got.at[1, j],
            has_last & (z == 0) if j == 0 else has_last,
            has_last & (z == 3) if j == 0 else has_last,
        )
        for j in range(2)
    ]
    bulk = [
        Route(sems, 6 + n, at.sibling, dq_sent.at[n], dq_got.at[n]) for n in range(2)
    ]
    back = [
        Route(sems, 8 + j, at.last, beside_sum.at[j], later_got.at[j], has_last, has_next)
        for j in range(2)
    ]
    far_up = Route(sems, 10, at.above, far_sum.at[0], far_got.at[0])
    far_down = Route(sems, 11, at.below, far_sum.at[1], far_got.at[1])
    near_up_0 = Route(sems, 12, at.above, near_sum.at[0], near_got.at[0])
    near_up_1 = Route(sems, 13, at.above, given(OWN, up, 1), near_got.at[1], z == 3, z == 0)
    near_down_0 = Route(sems, 14, at.below, given(OWN, down, 0), near_got.at[2])
    near_down_1 = Route(sems, 15, at.below, near_sum.at[1], near_got.at[3])

    load.wait()
    for copy in (side_down[1], side_up[1], far_back[1], side_up[0], side_down[0], far_back[0]):
        copy.start()
    load_dq.wait()
    for copy in bulk:
        copy.start()
    load_own.wait()
    for copy in loads:
        copy.wait()
    ends = doc_ends(docs_ref)
    tile = at.column * 16 * B + (z + 4 * core) * 2 * B
    dka[...] = jnp.zeros_like(dka)
    dva[...] = jnp.zeros_like(dva)

    def diagonal(n):
        block, b = (n + 1) // 2, n // 2
        here = pl.ds(pl.multiple_of(block * B, B), B)
        there = pl.ds(pl.multiple_of(b * B, B), B)
        pos = positions(tile + block * B)
        bias[...] = hidden(tile + b * B, doc_start(ends, pos), pos)
        dk, dv, dq = gradients(
            k_ref[there],
            v_ref[there],
            [q_ref[here, h * W : (h + 1) * W] for h in range(heads)],
            [g_ref[here, h * W : (h + 1) * W] for h in range(heads)],
            [stat[0, h : h + 1, here] for h in range(heads)],
            [stat[1, h : h + 1, here] for h in range(heads)],
            bias,
        )
        dka[b] += dk
        dva[b] += dv
        dqt[block] += dq

    pl.loop(0, 3)(diagonal)

    @pl.when(has_last)
    def _():
        for copy in side_up + side_down:
            copy.arrived()
        for j in range(2):
            final[j] = held(BEFORE, z, j)
        final[1] += beside_got[0, 1].astype(jnp.float32) + beside_got[1, 1].astype(jnp.float32)

        @pl.when(z != 0)
        def _():
            final[0] += beside_got[0, 0].astype(jnp.float32)

        @pl.when(z == 3)
        def _():
            final[0] += beside_got[1, 0].astype(jnp.float32)

        beside_sum[...] = final[...].astype(jnp.bfloat16)
        for copy in back:
            copy.start()

    def add_across(j):
        far_back[j].make(across_got.at[j]).wait_recv()
        final[j] += across_got[j].astype(jnp.float32)

    for j in range(2):
        final[j] = held(OWN, across, j)
        pl.when(far_back[j].gets)(functools.partial(add_across, j))
        far_sum[j] = final[j].astype(jnp.bfloat16)
    for copy in (far_up, far_down, near_down_0, near_up_1):
        copy.start()
    for copy in bulk:
        copy.arrived()
    eye = identity(B)
    for block in range(2):
        for h in range(heads):
            rows = slice(h * B, (h + 1) * B)
            total = dqt[block, :, rows] + dq_got[block, :, rows].astype(jnp.float32)
            rounded = (total * (1.0 / math.sqrt(W))).astype(jnp.bfloat16)
            turned = nt(eye, rounded).astype(jnp.bfloat16)
            dq_out[block * B : (block + 1) * B, h * W : (h + 1) * W] = turned
    out_q = pltpu.make_async_copy(dq_out, dq_hbm, put.at[0])
    out_q.start()
    far_up.arrived()
    near_sum[0] = (held(OWN, up, 0) + far_got[0].astype(jnp.float32)).astype(jnp.bfloat16)
    near_up_0.start()
    far_down.arrived()
    near_sum[1] = (held(OWN, down, 1) + far_got[1].astype(jnp.float32)).astype(jnp.bfloat16)
    near_down_1.start()
    near_down_0.arrived()
    near_up_0.arrived()
    final[0] = (
        held(OWN, z, 0) + near_got[0].astype(jnp.float32) + near_got[2].astype(jnp.float32)
    )
    near_down_1.arrived()
    final[1] = held(OWN, z, 1) + near_got[3].astype(jnp.float32)

    @pl.when(z == 0)
    def _():
        near_up_1.make(near_got.at[1]).wait_recv()
        final[1] += near_got[1].astype(jnp.float32)

    @pl.when(has_next)
    def _():
        for j in range(2):
            back[j].make(later_got.at[j]).wait_recv()
            final[j] += later_got[j].astype(jnp.float32)

    given_half[...] = final[1 - core].astype(jnp.bfloat16)
    give_k = Route(sems, 16, at.sibling, given_half.at[0], dk_ref.at[B:])
    give_v = Route(sems, 17, at.sibling, given_half.at[1], dv_ref.at[B:])
    give_k.start()
    give_v.start()
    scale = 1.0 / math.sqrt(W)
    dk_ref[:B] = (final[core, 0] + dka[0] * scale).astype(jnp.bfloat16)
    dv_ref[:B] = (final[core, 1] + dva[0]).astype(jnp.bfloat16)
    give_k.arrived()
    give_v.arrived()
    dk_ref[B:] = (dk_ref[B:].astype(jnp.float32) + dka[1] * scale).astype(jnp.bfloat16)
    dv_ref[B:] = (dv_ref[B:].astype(jnp.float32) + dva[1]).astype(jnp.bfloat16)
    out_k = pltpu.make_async_copy(dk_ref, dk_hbm, put.at[1])
    out_v = pltpu.make_async_copy(dv_ref, dv_hbm, put.at[2])
    out_k.start()
    out_v.start()
    for copy in (out_q, out_k, out_v):
        copy.wait()
    for copy in (
        far_back + side_up + side_down + bulk + back
        + [far_up, far_down, near_up_0, near_up_1, near_down_0, near_down_1, give_k, give_v]
    ):
        copy.sent()


def give_back(columns, docs, q, k, v, g, stat, dq_own, dq_other, part):
    rows, features = q.shape
    heads = features // W
    some = pl.BlockSpec(memory_space=pl.ANY)
    vmem = pl.BlockSpec(memory_space=pltpu.VMEM)
    block = (2, B, W)
    return pl.pallas_call(
        functools.partial(return_kernel, columns, heads),
        out_shape=(
            jax.ShapeDtypeStruct((rows, features), jnp.bfloat16),
            jax.ShapeDtypeStruct((rows, W), jnp.bfloat16),
            jax.ShapeDtypeStruct((rows, W), jnp.bfloat16),
        ),
        in_specs=[vmem] + [some] * 8,
        out_specs=(some,) * 3,
        scratch_shapes=[
            pltpu.VMEM(q.shape, q.dtype),
            pltpu.VMEM(k.shape, k.dtype),
            pltpu.VMEM(v.shape, v.dtype),
            pltpu.VMEM(g.shape, g.dtype),
            pltpu.VMEM(stat.shape[1:], stat.dtype),
            pltpu.VMEM(dq_own.shape, dq_own.dtype),
            pltpu.VMEM(dq_other.shape, dq_other.dtype),
            pltpu.VMEM(dq_other.shape, dq_other.dtype),
            pltpu.VMEM(q.shape, jnp.bfloat16),
            pltpu.VMEM((rows, W), jnp.bfloat16),
            pltpu.VMEM((rows, W), jnp.bfloat16),
            pltpu.VMEM((2, B, W), jnp.float32),
            pltpu.VMEM((2, B, W), jnp.float32),
            pltpu.VMEM((B, B), jnp.float32),
            pltpu.VMEM((16, *block), jnp.bfloat16),
            pltpu.VMEM((2, *block), jnp.bfloat16),
            pltpu.VMEM((2, 2, *block), jnp.bfloat16),
            pltpu.VMEM((2, *block), jnp.bfloat16),
            pltpu.VMEM((2, *block), jnp.bfloat16),
            pltpu.VMEM((2, *block), jnp.bfloat16),
            pltpu.VMEM((2, *block), jnp.bfloat16),
            pltpu.VMEM((2, *block), jnp.bfloat16),
            pltpu.VMEM((4, *block), jnp.bfloat16),
            pltpu.VMEM((2, *block), jnp.float32),
            pltpu.VMEM(block, jnp.bfloat16),
            pltpu.SemaphoreType.DMA((9,)),
            pltpu.SemaphoreType.DMA((3,)),
            pltpu.SemaphoreType.DMA((18,)),
            pltpu.SemaphoreType.DMA((18,)),
        ],
        compiler_params=pltpu.CompilerParams(
            collective_id=1, has_side_effects=True, vmem_limit_bytes=VMEM
        ),
    )(docs, q, k, v, g, stat, dq_own, dq_other, part)


def publish_kernel(*refs):
    sources, targets, held, get, put = refs[:3], refs[3:6], refs[6:9], refs[9], refs[10]
    pieces = []
    for source, target, mid in zip(sources, targets, held):
        rows = min(source.shape[0], 128 * 1024 // source.shape[1])
        for at in range(0, source.shape[0], rows):
            here = slice(at, at + rows)
            n = len(pieces)
            pieces.append(
                (
                    pltpu.make_async_copy(source.at[here], mid.at[here], get.at[n]),
                    pltpu.make_async_copy(mid.at[here], target.at[here], put.at[n]),
                )
            )
    for into, _ in pieces:
        into.start()
    for into, out in pieces:
        into.wait()
        out.start()
    for _, out in pieces:
        out.wait()


def publish(*results):
    some = pl.BlockSpec(memory_space=pl.ANY)
    return pl.pallas_call(
        publish_kernel,
        out_shape=tuple(jax.ShapeDtypeStruct(x.shape, x.dtype) for x in results),
        in_specs=[some] * 3,
        out_specs=(some,) * 3,
        scratch_shapes=[pltpu.VMEM(x.shape, x.dtype) for x in results]
        + [pltpu.SemaphoreType.DMA((6,))] * 2,
        compiler_params=pltpu.CompilerParams(vmem_limit_bytes=VMEM),
    )(*results)


def solution(mesh):
    columns = mesh.shape["ctx"] // 2

    def on_device(q, k, v, o, g, log_total, doc_lengths):
        docs = doc_lengths[None, :]
        q_other, g_other, stat, window, dq, sums = gather(columns, docs, q, g, o, k, v, log_total)
        dq_own, dq_other, part = attend(docs, q, q_other, g, g_other, stat, window, dq, sums)
        dq, dk, dv = give_back(columns, docs, q, k, v, g, stat, dq_own, dq_other, part)
        return publish(dq, dk, dv)

    rows = P(("ctx", "section"), None)
    return jax.shard_map(
        on_device,
        mesh=mesh,
        in_specs=(rows, rows, rows, rows, rows, P(None, ("ctx", "section")), P()),
        out_specs=(rows, rows, rows),
        check_vma=False,
    )
```

profile of v0, /device:TPU:19, one launch (start us, length us, event | category | flops | bytes accessed | tf_op | source)
XLA Modules:
  0.0 77.3 jit_solution(12419753530284580651)
XLA Ops:
  0.6 25.1 %shard_map.94 = (bf16[512,1024]{1,0:T(8,128)(2,1)}, bf16[512,1024]{1,0:T(8,128)(2,1)}, f32[2,2,8,512]{3,2,1,0:T(8,128)}, bf16[16,2,256,128]{3,2,1,0:T(8,128)(2,1...) custom-call(s32[1,128]{1,0:T(1,128)} %bitcast.1, bf16[512,1024]{1,0:T(8,128)(2,1)} %q_hbm.1, ...), custom_call_target="tpu_custom_call" | custom-call | tf_op jit(solution)/shard_map/pallas_call | solution.py:354
  25.7 25.4 %shard_map.95 = (f32[2,128,2048]{2,1,0:T(8,128)}, bf16[2,128,2048]{2,1,0:T(8,128)(2,1)}, bf16[16,2,256,128]{3,2,1,0:T(8,128)(2,1)}) custom-call(s32[1,128]{1,0:T(1,128)} %bitcast.2, bf16[512,1024]{1,0:T(8,128)(2,1)} %q_hbm.1, bf16[512,1024]{1,0:T(8,128)(2,1)} %get-tuple-element.16.qb_hbm, bf16[512,1024]{1,0:T(8,128)(2,1)} %g_hbm.1, ...), custom_call_target="tpu_custom_call" | custom-call | flops 13421772800 | bytes 16777216 | tf_op jit(solution)/shard_map/pallas_call | solution.py:523
  51.1 23.9 %shard_map.96 = (bf16[512,1024]{1,0:T(8,128)(2,1)}, bf16[512,128]{1,0:T(8,128)(2,1)}, bf16[512,128]{1,0:T(8,128)(2,1)}) custom-call(s32[1,128]{1,0:T(1,128)} %bitcast.3, bf16[512,1024]{1,0:T(8,128)(2,1)} %q_hbm.1, bf16[512,128]{1,0:T(8,128)(2,1)} %k_hbm.1, bf16[512,128]{1,0:T(8,128)(2,1)} %v_hbm.1, bf16[512,1024]{1,0:T(8,128)(2,1)} %g_hbm.1, ...), custom_call_target="tpu_custom_call" | custom-call | tf_op jit(solution)/shard_map/pallas_call | solution.py:763
  75.0 2.1 %shard_map.97 = (bf16[512,1024]{1,0:T(8,128)(2,1)}, bf16[512,128]{1,0:T(8,128)(2,1)}, bf16[512,128]{1,0:T(8,128)(2,1)}) custom-call(bf16[512,1024]{1,0:T(8,128)(2,1)} %get-tuple-element.24.refs_0_, bf16[512,128]{1,0:T(8,128)(2,1)} %get-tuple-element.25.refs_1_, bf16[512,128]{1,0:T(8,128)(2,1)} %get-tuple-element.26.refs_2_), custom_call_target="tpu_custom_call" | custom-call | tf_op jit(solution)/shard_map/pallas_call | solution.py:834
where the time goes:
time: 77.4 us; the launch traced here: 77.3 us
  Pallas kernels  76.5 us (99%)
  between operations  0.81 us (1%)
    pallas_call x1, Pallas kernels, attend(): pl.pallas_call(functools.partial(attend_kernel, heads), out_shape=(jax.Sh...  25.4 us
    pallas_call x1, Pallas kernels, gather(): pl.pallas_call(functools.partial(gather_kernel, columns, heads), out_shap...  25.1 us
    pallas_call x1, Pallas kernels, give_back(): pl.pallas_call(functools.partial(return_kernel, columns, heads), out_shap...  23.9 us
    pallas_call x1, Pallas kernels, publish(): pl.pallas_call(publish_kernel, out_shape=tuple((jax.ShapeDtypeStruct(x.sh...  2.1 us

commit v1 on v0

--- a/solution.py
+++ b/solution.py
@@ -293,12 +293,19 @@
         )
     ]
 
+    def sibling_here():
+        for copy in bulk:
+            copy.arrived()
+        stats.arrived()
+
+    flip = (core == 0) & (z == 0)
+
     @pl.loop(0, 4)
     def _(n):
         @pl.when(n == 0)
         def _():
             up_0.arrived()
-            pl.when((core == 0) & (z == 0))(before_up_1.arrived)
+            pl.when(flip)(sibling_here)
 
         @pl.when(n == 1)
         def _():
@@ -310,14 +317,12 @@
         @pl.when(n == 2)
         def _():
             down_1.arrived()
-            for copy in bulk:
-                copy.arrived()
-            stats.arrived()
-            pl.when((core == 1) & (z == 0))(before_up_1.arrived)
-            for copy in puts[:5]:
+            pl.when(jnp.logical_not(flip))(sibling_here)
+            pl.when(z == 0)(before_up_1.arrived)
+            for copy in puts[:4]:
                 copy.start()
 
-        side, part = n // 2, n % 2
+        side, part = jnp.where(flip, 1 - n // 2, n // 2), n % 2
 
         @pl.when(side == core)
         def _():
@@ -327,8 +332,8 @@
         def _():
             near(side, part, z + 4, [slot(OWN, z, 0), near_4], [z, z + 3], 0)
 
-    puts[6].start()
-    puts[7].start()
+    for copy in (puts[4], puts[6], puts[7]):
+        copy.start()
     pl.when(z != 0)(before_up_1.arrived)
     for copy in (before_up_0, before_down_0, before_down_1, next_far_0, next_far_1):
         copy.arrived()
@@ -398,7 +403,6 @@
                 (stat_hbm, stat_ref),
                 (window_hbm.at[:8], window_ref.at[:8]), (window_hbm.at[8:], window_ref.at[8:]),
                 (kv_hbm, dkv), (qa_hbm, q_ref.at[0]), (ga_hbm, g_ref.at[0]),
-                (dq_hbm.at[:2], dqt.at[:2]),
                 (qb_hbm, q_ref.at[1]), (gb_hbm, g_ref.at[1]), (dq_hbm.at[2:], dqt.at[2:]),
             )
         )
@@ -427,7 +431,8 @@
         bounds[1, block] = jnp.where(last % (2 * B) > half_of(b) * B, b + 1, b)
     dka[...] = jnp.zeros_like(dka)
     dva[...] = jnp.zeros_like(dva)
-    for load in loads[:7]:
+    dqt[:2] = jnp.zeros((2, *dqt.shape[1:]), dqt.dtype)
+    for load in loads[:6]:
         load.wait()
     down = lax.rem(z + 3, 4)
     nears = (
@@ -446,7 +451,7 @@
 
         @pl.when(block == 2)
         def _():
-            for load in loads[7:]:
+            for load in loads[6:]:
                 load.wait()
 
         def work(blocks, mask=None):
@@ -543,7 +548,7 @@
             pltpu.VMEM((B, B), jnp.float32),
             pltpu.VMEM((4, 1, B), jnp.float32),
             pltpu.SMEM((2, 4), jnp.int32),
-            pltpu.SemaphoreType.DMA((10,)),
+            pltpu.SemaphoreType.DMA((9,)),
             pltpu.SemaphoreType.DMA((20,)),
         ],
         compiler_params=pltpu.CompilerParams(vmem_limit_bytes=VMEM),
@@ -554,9 +559,9 @@
 
 
 def return_kernel(
-    columns, heads, docs_ref, q_hbm, k_hbm, v_hbm, g_hbm, stat_hbm, dq_own, dq_other, part_ref,
+    columns, heads, docs_ref, q_hbm, k_hbm, v_hbm, g_hbm, stat_hbm, dq_near, dq_own, dq_other, part_ref,
     dq_hbm, dk_hbm, dv_hbm,
-    q_ref, k_ref, v_ref, g_ref, stat, dqt, dq_sent, dq_got, dq_out, dk_ref, dv_ref, dka, dva, bias,
+    q_ref, k_ref, v_ref, g_ref, stat, dqt, dqn, dq_got, dq_out, dk_ref, dv_ref, dka, dva, bias,
     part, across_got, beside_got, beside_sum, later_got, far_got, far_sum, near_sum,
     near_got, final, given_half, local, put, send, recv,
 ):
@@ -565,7 +570,7 @@
     sems = (send, recv)
     load = pltpu.make_async_copy(part_ref.at[:8], part.at[:8], local.at[0])
     load_own = pltpu.make_async_copy(part_ref.at[8:], part.at[8:], local.at[1])
-    load_dq = pltpu.make_async_copy(dq_other, dq_sent, local.at[2])
+    load_dq = pltpu.make_async_copy(dq_near.at[:2], dqn, local.at[2])
     load.start()
     load_own.start()
     load_dq.start()
@@ -584,7 +589,7 @@
     has_next, has_last = at.has_next, at.has_last
 
     def given(side, zc, j):
-        return part.at[slot(side, zc, j)]
+        return part_ref.at[slot(side, zc, j)]
 
     def held(side, zc, j):
         return part[slot(side, zc, j)].astype(jnp.float32)
@@ -614,7 +619,7 @@
         for j in range(2)
     ]
     bulk = [
-        Route(sems, 6 + n, at.sibling, dq_sent.at[n], dq_got.at[n]) for n in range(2)
+        Route(sems, 6 + n, at.sibling, dq_other.at[n], dq_got.at[n]) for n in range(2)
     ]
     back = [
         Route(sems, 8 + j, at.last, beside_sum.at[j], later_got.at[j], has_last, has_next)
@@ -627,14 +632,11 @@
     near_down_0 = Route(sems, 14, at.below, given(OWN, down, 0), near_got.at[2])
     near_down_1 = Route(sems, 15, at.below, near_sum.at[1], near_got.at[3])
 
-    load.wait()
     for copy in (side_down[1], side_up[1], far_back[1], side_up[0], side_down[0], far_back[0]):
         copy.start()
-    load_dq.wait()
     for copy in bulk:
         copy.start()
-    load_own.wait()
-    for copy in loads:
+    for copy in (load, load_own, load_dq, *loads):
         copy.wait()
     ends = doc_ends(docs_ref)
     tile = at.column * 16 * B + (z + 4 * core) * 2 * B
@@ -698,7 +700,8 @@
     for block in range(2):
         for h in range(heads):
             rows = slice(h * B, (h + 1) * B)
-            total = dqt[block, :, rows] + dq_got[block, :, rows].astype(jnp.float32)
+            total = dqt[block, :, rows] + dqn[block, :, rows]
+            total = total + dq_got[block, :, rows].astype(jnp.float32)
             rounded = (total * (1.0 / math.sqrt(W))).astype(jnp.bfloat16)
             turned = nt(eye, rounded).astype(jnp.bfloat16)
             dq_out[block * B : (block + 1) * B, h * W : (h + 1) * W] = turned
@@ -754,7 +757,7 @@
         copy.sent()
 
 
-def give_back(columns, docs, q, k, v, g, stat, dq_own, dq_other, part):
+def give_back(columns, docs, q, k, v, g, stat, dq_near, dq_own, dq_other, part):
     rows, features = q.shape
     heads = features // W
     some = pl.BlockSpec(memory_space=pl.ANY)
@@ -767,7 +770,7 @@
             jax.ShapeDtypeStruct((rows, W), jnp.bfloat16),
             jax.ShapeDtypeStruct((rows, W), jnp.bfloat16),
         ),
-        in_specs=[vmem] + [some] * 8,
+        in_specs=[vmem] + [some] * 9,
         out_specs=(some,) * 3,
         scratch_shapes=[
             pltpu.VMEM(q.shape, q.dtype),
@@ -776,7 +779,7 @@
             pltpu.VMEM(g.shape, g.dtype),
             pltpu.VMEM(stat.shape[1:], stat.dtype),
             pltpu.VMEM(dq_own.shape, dq_own.dtype),
-            pltpu.VMEM(dq_other.shape, dq_other.dtype),
+            pltpu.VMEM(dq_own.shape, dq_own.dtype),
             pltpu.VMEM(dq_other.shape, dq_other.dtype),
             pltpu.VMEM(q.shape, jnp.bfloat16),
             pltpu.VMEM((rows, W), jnp.bfloat16),
@@ -803,7 +806,7 @@
         compiler_params=pltpu.CompilerParams(
             collective_id=1, has_side_effects=True, vmem_limit_bytes=VMEM
         ),
-    )(docs, q, k, v, g, stat, dq_own, dq_other, part)
+    )(docs, q, k, v, g, stat, dq_near, dq_own, dq_other, part)
 
 
 def publish_kernel(*refs):
@@ -849,7 +852,7 @@
         docs = doc_lengths[None, :]
         q_other, g_other, stat, window, dq, sums = gather(columns, docs, q, g, o, k, v, log_total)
         dq_own, dq_other, part = attend(docs, q, q_other, g, g_other, stat, window, dq, sums)
-        dq, dk, dv = give_back(columns, docs, q, k, v, g, stat, dq_own, dq_other, part)
+        dq, dk, dv = give_back(columns, docs, q, k, v, g, stat, dq, dq_own, dq_other, part)
         return publish(dq, dk, dv)
 
     rows = P(("ctx", "section"), None)

time: 77.4 us -> 82.1 us (1.061)
  the two profiles are of different devices: /device:TPU:19 before, /device:TPU:7 now
where the time goes in v1:
time: 82.1 us; the launch traced here: 81.9 us
  Pallas kernels  81.1 us (99%)
    pallas_call x1, Pallas kernels, give_back(): pl.pallas_call(functools.partial(return_kernel, columns, heads), out_shap...  44 us
    pallas_call x1, Pallas kernels, gather(): pl.pallas_call(functools.partial(gather_kernel, columns, heads), out_shap...  27.7 us
    pallas_call x1, Pallas kernels, attend(): pl.pallas_call(functools.partial(attend_kernel, heads), out_shape=(jax.Sh...  7.27 us
    pallas_call x1, Pallas kernels, publish(): pl.pallas_call(publish_kernel, out_shape=tuple((jax.ShapeDtypeStruct(x.sh...  2.1 us

profile of v1, /device:TPU:7, one launch (start us, length us, event | category | flops | bytes accessed | tf_op | source)
XLA Modules:
  0.0 81.9 jit_solution(14290452762933667470)
XLA Ops:
  0.6 27.7 %shard_map.94 = (bf16[512,1024]{1,0:T(8,128)(2,1)}, bf16[512,1024]{1,0:T(8,128)(2,1)}, f32[2,2,8,512]{3,2,1,0:T(8,128)}, bf16[16,2,256,128]{3,2,1,0:T(8,128)(2,1...) custom-call(s32[1,128]{1,0:T(1,128)} %bitcast.1, bf16[512,1024]{1,0:T(8,128)(2,1)} %q_hbm.1, ...), custom_call_target="tpu_custom_call" | custom-call | tf_op jit(solution)/shard_map/pallas_call | solution.py:359
  28.4 7.3 %shard_map.95 = (f32[2,128,2048]{2,1,0:T(8,128)}, bf16[2,128,2048]{2,1,0:T(8,128)(2,1)}, bf16[16,2,256,128]{3,2,1,0:T(8,128)(2,1)}) custom-call(s32[1,128]{1,0:T(1,128)} %bitcast.2, bf16[512,1024]{1,0:T(8,128)(2,1)} %q_hbm.1, bf16[512,1024]{1,0:T(8,128)(2,1)} %get-tuple-element.17.qb_hbm, bf16[512,1024]{1,0:T(8,128)(2,1)} %g_hbm.1, ...), custom_call_target="tpu_custom_call" | custom-call | flops 13421772800 | bytes 16777216 | tf_op jit(solution)/shard_map/pallas_call | solution.py:528
  35.6 44.0 %shard_map.96 = (bf16[512,1024]{1,0:T(8,128)(2,1)}, bf16[512,128]{1,0:T(8,128)(2,1)}, bf16[512,128]{1,0:T(8,128)(2,1)}) custom-call(s32[1,128]{1,0:T(1,128)} %bitcast.3, bf16[512,1024]{1,0:T(8,128)(2,1)} %q_hbm.1, bf16[512,128]{1,0:T(8,128)(2,1)} %k_hbm.1, bf16[512,128]{1,0:T(8,128)(2,1)} %v_hbm.1, bf16[512,1024]{1,0:T(8,128)(2,1)} %g_hbm.1, ...), custom_call_target="tpu_custom_call" | custom-call | tf_op jit(solution)/shard_map/pallas_call | solution.py:766
  79.7 2.1 %shard_map.97 = (bf16[512,1024]{1,0:T(8,128)(2,1)}, bf16[512,128]{1,0:T(8,128)(2,1)}, bf16[512,128]{1,0:T(8,128)(2,1)}) custom-call(bf16[512,1024]{1,0:T(8,128)(2,1)} %get-tuple-element.24.refs_0_, bf16[512,128]{1,0:T(8,128)(2,1)} %get-tuple-element.25.refs_1_, bf16[512,128]{1,0:T(8,128)(2,1)} %get-tuple-element.26.refs_2_), custom_call_target="tpu_custom_call" | custom-call | tf_op jit(solution)/shard_map/pallas_call | solution.py:837

commit v2 on v1

--- a/solution.py
+++ b/solution.py
@@ -95,7 +95,7 @@
         self.next_across = (self.next[0], self.across)
         self.last_across = (self.last[0], self.across)
 
-    def barrier(self, straight=False):
+    def barrier(self, to_next=(), to_last=(), expect=0):
         barrier = pltpu.get_barrier_semaphore()
 
         def greet(*devices):
@@ -103,12 +103,11 @@
                 pl.semaphore_signal(barrier, inc=1, device_id=device, device_id_type=MESH)
 
         greet(self.sibling, self.above, self.below)
-        later = (self.next, self.next_across) if straight else (self.next,)
-        earlier = (self.last, self.last_across) if straight else (self.last,)
-        pl.when(self.has_next)(lambda: greet(*later))
-        pl.when(self.has_last)(lambda: greet(*earlier))
-        columns = self.has_next.astype(jnp.int32) + self.has_last.astype(jnp.int32)
-        pl.semaphore_wait(barrier, 3 + len(later) * columns)
+        if to_next:
+            pl.when(self.has_next)(lambda: greet(*to_next))
+        if to_last:
+            pl.when(self.has_last)(lambda: greet(*to_last))
+        pl.semaphore_wait(barrier, 3 + expect)
 
 
 class Route:
@@ -163,7 +162,7 @@
     def _():
         window[slot(BEFORE, 3, 1)] = jnp.zeros((2, B, W), window.dtype)
 
-    at.barrier()
+    at.barrier(to_last=(at.last,), expect=at.has_next.astype(jnp.int32))
 
     theirs = window.at[slot(OWN, z, 1 - core)]
     swap_k = Route(sems, 0, at.sibling, k_own.at[B:], mine.at[0], arrival=theirs.at[0])
@@ -562,7 +561,7 @@
     columns, heads, docs_ref, q_hbm, k_hbm, v_hbm, g_hbm, stat_hbm, dq_near, dq_own, dq_other, part_ref,
     dq_hbm, dk_hbm, dv_hbm,
     q_ref, k_ref, v_ref, g_ref, stat, dqt, dqn, dq_got, dq_out, dk_ref, dv_ref, dka, dva, bias,
-    part, across_got, beside_got, beside_sum, later_got, far_got, far_sum, near_sum,
+    part, across_got, beside_got, beside_sum, later_got, far_got, near_sum,
     near_got, final, given_half, local, put, send, recv,
 ):
     at = Links(columns)
@@ -585,7 +584,9 @@
     ]
     for copy in loads:
         copy.start()
-    at.barrier()
+    at.barrier(
+        to_next=(at.next, at.next_across), expect=2 * at.has_last.astype(jnp.int32)
+    )
     has_next, has_last = at.has_next, at.has_last
 
     def given(side, zc, j):
@@ -596,9 +597,9 @@
 
     far_back = [
         Route(
-            sems, j, at.last, given(BEFORE, across, j), across_got.at[j],
+            sems, j, at.last_across, given(BEFORE, across, j), across_got.at[j],
             has_last & (z < 2) if j == 0 else has_last,
-            has_next & (z < 2) if j == 0 else has_next,
+            has_next & (z >= 2) if j == 0 else has_next,
         )
         for j in range(2)
     ]
@@ -625,19 +626,59 @@
         Route(sems, 8 + j, at.last, beside_sum.at[j], later_got.at[j], has_last, has_next)
         for j in range(2)
     ]
-    far_up = Route(sems, 10, at.above, far_sum.at[0], far_got.at[0])
-    far_down = Route(sems, 11, at.below, far_sum.at[1], far_got.at[1])
+    far_up = Route(sems, 10, at.above, given(OWN, across, 0), far_got.at[0])
+    far_down = Route(
+        sems, 11, at.below, given(OWN, across, 1), far_got.at[1], z >= 2, (z == 1) | (z == 2)
+    )
     near_up_0 = Route(sems, 12, at.above, near_sum.at[0], near_got.at[0])
     near_up_1 = Route(sems, 13, at.above, given(OWN, up, 1), near_got.at[1], z == 3, z == 0)
     near_down_0 = Route(sems, 14, at.below, given(OWN, down, 0), near_got.at[2])
-    near_down_1 = Route(sems, 15, at.below, near_sum.at[1], near_got.at[3])
-
-    for copy in (side_down[1], side_up[1], far_back[1], side_up[0], side_down[0], far_back[0]):
+    near_down_1 = Route(sems, 15, at.below, near_sum.at[1], near_got.at[3], z != 0, z != 3)
+
+    for copy in (side_down[1], side_up[1], side_up[0], side_down[0], far_back[1], far_back[0]):
         copy.start()
-    for copy in bulk:
+    for copy in (far_up, far_down, *bulk):
         copy.start()
     for copy in (load, load_own, load_dq, *loads):
         copy.wait()
+
+    @pl.when(has_last)
+    def _():
+        for copy in side_up + side_down:
+            copy.arrived()
+        for j in range(2):
+            final[j] = held(BEFORE, z, j)
+        final[1] += beside_got[0, 1].astype(jnp.float32) + beside_got[1, 1].astype(jnp.float32)
+
+        @pl.when(z != 0)
+        def _():
+            final[0] += beside_got[0, 0].astype(jnp.float32)
+
+        @pl.when(z == 3)
+        def _():
+            final[0] += beside_got[1, 0].astype(jnp.float32)
+
+        beside_sum[...] = final[...].astype(jnp.bfloat16)
+        for copy in back:
+            copy.start()
+
+    for copy in (near_down_0, near_up_1):
+        copy.start()
+    far_up.arrived()
+    near_sum[0] = (held(OWN, up, 0) + far_got[0].astype(jnp.float32)).astype(jnp.bfloat16)
+    near_up_0.start()
+
+    @pl.when((z == 1) | (z == 2))
+    def _():
+        far_down.make(far_got.at[1]).wait_recv()
+        total = held(OWN, down, 1) + far_got[1].astype(jnp.float32)
+        near_sum[1] = total.astype(jnp.bfloat16)
+
+    @pl.when(z == 3)
+    def _():
+        near_sum[1] = part[slot(OWN, down, 1)]
+
+    near_down_1.start()
     ends = doc_ends(docs_ref)
     tile = at.column * 16 * B + (z + 4 * core) * 2 * B
     dka[...] = jnp.zeros_like(dka)
@@ -663,37 +704,6 @@
         dqt[block] += dq
 
     pl.loop(0, 3)(diagonal)
-
-    @pl.when(has_last)
-    def _():
-        for copy in side_up + side_down:
-            copy.arrived()
-        for j in range(2):
-            final[j] = held(BEFORE, z, j)
-        final[1] += beside_got[0, 1].astype(jnp.float32) + beside_got[1, 1].astype(jnp.float32)
-
-        @pl.when(z != 0)
-        def _():
-            final[0] += beside_got[0, 0].astype(jnp.float32)
-
-        @pl.when(z == 3)
-        def _():
-            final[0] += beside_got[1, 0].astype(jnp.float32)
-
-        beside_sum[...] = final[...].astype(jnp.bfloat16)
-        for copy in back:
-            copy.start()
-
-    def add_across(j):
-        far_back[j].make(across_got.at[j]).wait_recv()
-        final[j] += across_got[j].astype(jnp.float32)
-
-    for j in range(2):
-        final[j] = held(OWN, across, j)
-        pl.when(far_back[j].gets)(functools.partial(add_across, j))
-        far_sum[j] = final[j].astype(jnp.bfloat16)
-    for copy in (far_up, far_down, near_down_0, near_up_1):
-        copy.start()
     for copy in bulk:
         copy.arrived()
     eye = identity(B)
@@ -707,24 +717,32 @@
             dq_out[block * B : (block + 1) * B, h * W : (h + 1) * W] = turned
     out_q = pltpu.make_async_copy(dq_out, dq_hbm, put.at[0])
     out_q.start()
-    far_up.arrived()
-    near_sum[0] = (held(OWN, up, 0) + far_got[0].astype(jnp.float32)).astype(jnp.bfloat16)
-    near_up_0.start()
-    far_down.arrived()
-    near_sum[1] = (held(OWN, down, 1) + far_got[1].astype(jnp.float32)).astype(jnp.bfloat16)
-    near_down_1.start()
     near_down_0.arrived()
     near_up_0.arrived()
     final[0] = (
         held(OWN, z, 0) + near_got[0].astype(jnp.float32) + near_got[2].astype(jnp.float32)
     )
-    near_down_1.arrived()
-    final[1] = held(OWN, z, 1) + near_got[3].astype(jnp.float32)
+    final[1] = held(OWN, z, 1)
 
     @pl.when(z == 0)
     def _():
         near_up_1.make(near_got.at[1]).wait_recv()
         final[1] += near_got[1].astype(jnp.float32)
+
+    @pl.when(z != 3)
+    def _():
+        near_down_1.make(near_got.at[3]).wait_recv()
+        final[1] += near_got[3].astype(jnp.float32)
+
+    @pl.when(has_next)
+    def _():
+        far_back[1].make(across_got.at[1]).wait_recv()
+        final[1] += across_got[1].astype(jnp.float32)
+
+    @pl.when(has_next & (z >= 2))
+    def _():
+        far_back[0].make(across_got.at[0]).wait_recv()
+        final[0] += across_got[0].astype(jnp.float32)
 
     @pl.when(has_next)
     def _():
@@ -794,7 +812,6 @@
             pltpu.VMEM((2, *block), jnp.bfloat16),
             pltpu.VMEM((2, *block), jnp.bfloat16),
             pltpu.VMEM((2, *block), jnp.bfloat16),
-            pltpu.VMEM((2, *block), jnp.bfloat16),
             pltpu.VMEM((4, *block), jnp.bfloat16),
             pltpu.VMEM((2, *block), jnp.float32),
             pltpu.VMEM(block, jnp.bfloat16),

time: 82.1 us -> 78.6 us (0.957)
  the two profiles are of different devices: /device:TPU:7 before, /device:TPU:5 now
where the time goes in v2:
time: 78.6 us; the launch traced here: 78.5 us
  Pallas kernels  77.6 us (99%)
  between operations  0.81 us (1%)
    pallas_call x1, Pallas kernels, gather(): pl.pallas_call(functools.partial(gather_kernel, columns, heads), out_shap...  27.6 us
    pallas_call x1, Pallas kernels, give_back(): pl.pallas_call(functools.partial(return_kernel, columns, heads), out_shap...  27.4 us
    pallas_call x1, Pallas kernels, attend(): pl.pallas_call(functools.partial(attend_kernel, heads), out_shape=(jax.Sh...  20.6 us
    pallas_call x1, Pallas kernels, publish(): pl.pallas_call(publish_kernel, out_shape=tuple((jax.ShapeDtypeStruct(x.sh...  2.1 us

profile of v2, /device:TPU:5, one launch (start us, length us, event | category | flops | bytes accessed | tf_op | source)
XLA Modules:
  0.0 78.5 jit_solution(10518900017051026180)
XLA Ops:
  0.6 27.6 %shard_map.94 = (bf16[512,1024]{1,0:T(8,128)(2,1)}, bf16[512,1024]{1,0:T(8,128)(2,1)}, f32[2,2,8,512]{3,2,1,0:T(8,128)}, bf16[16,2,256,128]{3,2,1,0:T(8,128)(2,1...) custom-call(s32[1,128]{1,0:T(1,128)} %bitcast.1, bf16[512,1024]{1,0:T(8,128)(2,1)} %q_hbm.1, ...), custom_call_target="tpu_custom_call" | custom-call | tf_op jit(solution)/shard_map/pallas_call | solution.py:358
  28.2 20.6 %shard_map.95 = (f32[2,128,2048]{2,1,0:T(8,128)}, bf16[2,128,2048]{2,1,0:T(8,128)(2,1)}, bf16[16,2,256,128]{3,2,1,0:T(8,128)(2,1)}) custom-call(s32[1,128]{1,0:T(1,128)} %bitcast.2, bf16[512,1024]{1,0:T(8,128)(2,1)} %q_hbm.1, bf16[512,1024]{1,0:T(8,128)(2,1)} %get-tuple-element.17.qb_hbm, bf16[512,1024]{1,0:T(8,128)(2,1)} %g_hbm.1, ...), custom_call_target="tpu_custom_call" | custom-call | flops 13421772800 | bytes 16777216 | tf_op jit(solution)/shard_map/pallas_call | solution.py:527
  48.8 27.4 %shard_map.96 = (bf16[512,1024]{1,0:T(8,128)(2,1)}, bf16[512,128]{1,0:T(8,128)(2,1)}, bf16[512,128]{1,0:T(8,128)(2,1)}) custom-call(s32[1,128]{1,0:T(1,128)} %bitcast.3, bf16[512,1024]{1,0:T(8,128)(2,1)} %q_hbm.1, bf16[512,128]{1,0:T(8,128)(2,1)} %k_hbm.1, bf16[512,128]{1,0:T(8,128)(2,1)} %v_hbm.1, bf16[512,1024]{1,0:T(8,128)(2,1)} %g_hbm.1, ...), custom_call_target="tpu_custom_call" | custom-call | tf_op jit(solution)/shard_map/pallas_call | solution.py:784
  76.2 2.1 %shard_map.97 = (bf16[512,1024]{1,0:T(8,128)(2,1)}, bf16[512,128]{1,0:T(8,128)(2,1)}, bf16[512,128]{1,0:T(8,128)(2,1)}) custom-call(bf16[512,1024]{1,0:T(8,128)(2,1)} %get-tuple-element.24.refs_0_, bf16[512,128]{1,0:T(8,128)(2,1)} %get-tuple-element.25.refs_1_, bf16[512,128]{1,0:T(8,128)(2,1)} %get-tuple-element.26.refs_2_), custom_call_target="tpu_custom_call" | custom-call | tf_op jit(solution)/shard_map/pallas_call | solution.py:854

commit v3 on v1

--- a/solution.py
+++ b/solution.py
@@ -92,10 +92,8 @@
         self.has_last = self.column > 0
         self.next = (jnp.where(self.has_next, ctx + 2, ctx), self.z)
         self.last = (jnp.where(self.has_last, ctx - 2, ctx), self.z)
-        self.next_across = (self.next[0], self.across)
-        self.last_across = (self.last[0], self.across)
-
-    def barrier(self, straight=False):
+
+    def barrier(self, to_next=(), to_last=(), expect=0):
         barrier = pltpu.get_barrier_semaphore()
 
         def greet(*devices):
@@ -103,12 +101,11 @@
                 pl.semaphore_signal(barrier, inc=1, device_id=device, device_id_type=MESH)
 
         greet(self.sibling, self.above, self.below)
-        later = (self.next, self.next_across) if straight else (self.next,)
-        earlier = (self.last, self.last_across) if straight else (self.last,)
-        pl.when(self.has_next)(lambda: greet(*later))
-        pl.when(self.has_last)(lambda: greet(*earlier))
-        columns = self.has_next.astype(jnp.int32) + self.has_last.astype(jnp.int32)
-        pl.semaphore_wait(barrier, 3 + len(later) * columns)
+        if to_next:
+            pl.when(self.has_next)(lambda: greet(*to_next))
+        if to_last:
+            pl.when(self.has_last)(lambda: greet(*to_last))
+        pl.semaphore_wait(barrier, 3 + expect)
 
 
 class Route:
@@ -163,7 +160,7 @@
     def _():
         window[slot(BEFORE, 3, 1)] = jnp.zeros((2, B, W), window.dtype)
 
-    at.barrier()
+    at.barrier(to_last=(at.last,), expect=at.has_next.astype(jnp.int32))
 
     theirs = window.at[slot(OWN, z, 1 - core)]
     swap_k = Route(sems, 0, at.sibling, k_own.at[B:], mine.at[0], arrival=theirs.at[0])
@@ -493,9 +490,17 @@
             bias[...] = jnp.where(kpos >= starts[block], 0.0, -jnp.inf)
             work([b], bias)
 
-        @pl.loop(0, (end - jnp.maximum(low, cut)) // 2)
+        pairs = jnp.maximum(end - jnp.maximum(low, cut), 0) // 2
+        odd = pairs % 2
+
+        @pl.loop(0, odd)
         def _(n):
-            work([real(cut + 2 * n), real(cut + 2 * n + 1)])
+            work([real(cut), real(cut + 1)])
+
+        @pl.loop(0, pairs // 2)
+        def _(n):
+            first = cut + 2 * odd + 4 * n
+            work([real(first + m) for m in range(4)])
 
         @pl.when(side == 0)
         def _():
@@ -585,7 +590,7 @@
     ]
     for copy in loads:
         copy.start()
-    at.barrier()
+    at.barrier(to_next=(at.next,), expect=at.has_last.astype(jnp.int32))
     has_next, has_last = at.has_next, at.has_last
 
     def given(side, zc, j):

time: 82.1 us -> 77 us (0.938)
  the two profiles are of different devices: /device:TPU:7 before, /device:TPU:11 now
where the time goes in v3:
time: 77 us; the launch traced here: 76.8 us
  Pallas kernels  76 us (99%)
  between operations  0.81 us (1%)
    pallas_call x1, Pallas kernels, gather(): pl.pallas_call(functools.partial(gather_kernel, columns, heads), out_shap...  26 us
    pallas_call x1, Pallas kernels, attend(): pl.pallas_call(functools.partial(attend_kernel, heads), out_shape=(jax.Sh...  24.5 us
    pallas_call x1, Pallas kernels, give_back(): pl.pallas_call(functools.partial(return_kernel, columns, heads), out_shap...  23.4 us
    pallas_call x1, Pallas kernels, publish(): pl.pallas_call(publish_kernel, out_shape=tuple((jax.ShapeDtypeStruct(x.sh...  2.1 us

profile of v3, /device:TPU:11, one launch (start us, length us, event | category | flops | bytes accessed | tf_op | source)
XLA Modules:
  0.0 76.8 jit_solution(1282011611440702512)
XLA Ops:
  0.6 26.0 %shard_map.94 = (bf16[512,1024]{1,0:T(8,128)(2,1)}, bf16[512,1024]{1,0:T(8,128)(2,1)}, f32[2,2,8,512]{3,2,1,0:T(8,128)}, bf16[16,2,256,128]{3,2,1,0:T(8,128)(2,1...) custom-call(s32[1,128]{1,0:T(1,128)} %bitcast.1, bf16[512,1024]{1,0:T(8,128)(2,1)} %q_hbm.1, ...), custom_call_target="tpu_custom_call" | custom-call | tf_op jit(solution)/shard_map/pallas_call | solution.py:356
  26.7 24.5 %shard_map.95 = (f32[2,128,2048]{2,1,0:T(8,128)}, bf16[2,128,2048]{2,1,0:T(8,128)(2,1)}, bf16[16,2,256,128]{3,2,1,0:T(8,128)(2,1)}) custom-call(s32[1,128]{1,0:T(1,128)} %bitcast.2, bf16[512,1024]{1,0:T(8,128)(2,1)} %q_hbm.1, bf16[512,1024]{1,0:T(8,128)(2,1)} %get-tuple-element.17.qb_hbm, bf16[512,1024]{1,0:T(8,128)(2,1)} %g_hbm.1, ...), custom_call_target="tpu_custom_call" | custom-call | flops 13421772800 | bytes 16777216 | tf_op jit(solution)/shard_map/pallas_call | solution.py:533
  51.2 23.4 %shard_map.96 = (bf16[512,1024]{1,0:T(8,128)(2,1)}, bf16[512,128]{1,0:T(8,128)(2,1)}, bf16[512,128]{1,0:T(8,128)(2,1)}) custom-call(s32[1,128]{1,0:T(1,128)} %bitcast.3, bf16[512,1024]{1,0:T(8,128)(2,1)} %q_hbm.1, bf16[512,128]{1,0:T(8,128)(2,1)} %k_hbm.1, bf16[512,128]{1,0:T(8,128)(2,1)} %v_hbm.1, bf16[512,1024]{1,0:T(8,128)(2,1)} %g_hbm.1, ...), custom_call_target="tpu_custom_call" | custom-call | tf_op jit(solution)/shard_map/pallas_call | solution.py:771
  74.6 2.1 %shard_map.97 = (bf16[512,1024]{1,0:T(8,128)(2,1)}, bf16[512,128]{1,0:T(8,128)(2,1)}, bf16[512,128]{1,0:T(8,128)(2,1)}) custom-call(bf16[512,1024]{1,0:T(8,128)(2,1)} %get-tuple-element.24.refs_0_, bf16[512,128]{1,0:T(8,128)(2,1)} %get-tuple-element.25.refs_1_, bf16[512,128]{1,0:T(8,128)(2,1)} %get-tuple-element.26.refs_2_), custom_call_target="tpu_custom_call" | custom-call | tf_op jit(solution)/shard_map/pallas_call | solution.py:842

commit v4 on v3

--- a/solution.py
+++ b/solution.py
@@ -565,8 +565,8 @@
 
 def return_kernel(
     columns, heads, docs_ref, q_hbm, k_hbm, v_hbm, g_hbm, stat_hbm, dq_near, dq_own, dq_other, part_ref,
-    dq_hbm, dk_hbm, dv_hbm,
-    q_ref, k_ref, v_ref, g_ref, stat, dqt, dqn, dq_got, dq_out, dk_ref, dv_ref, dka, dva, bias,
+    dq_hbm, own_hbm, got_hbm, rest_hbm,
+    q_ref, k_ref, v_ref, g_ref, stat, dqt, dqn, dq_got, dq_out, own_half, rest, dka, dva, bias,
     part, across_got, beside_got, beside_sum, later_got, far_got, far_sum, near_sum,
     near_got, final, given_half, local, put, send, recv,
 ):
@@ -668,6 +668,11 @@
         dqt[block] += dq
 
     pl.loop(0, 3)(diagonal)
+    scale = 1.0 / math.sqrt(W)
+    rest[0] = dka[1] * scale
+    rest[1] = dva[1]
+    out_rest = pltpu.make_async_copy(rest, rest_hbm, put.at[2])
+    out_rest.start()
 
     @pl.when(has_last)
     def _():
@@ -738,26 +743,18 @@
             final[j] += later_got[j].astype(jnp.float32)
 
     given_half[...] = final[1 - core].astype(jnp.bfloat16)
-    give_k = Route(sems, 16, at.sibling, given_half.at[0], dk_ref.at[B:])
-    give_v = Route(sems, 17, at.sibling, given_half.at[1], dv_ref.at[B:])
-    give_k.start()
-    give_v.start()
-    scale = 1.0 / math.sqrt(W)
-    dk_ref[:B] = (final[core, 0] + dka[0] * scale).astype(jnp.bfloat16)
-    dv_ref[:B] = (final[core, 1] + dva[0]).astype(jnp.bfloat16)
-    give_k.arrived()
-    give_v.arrived()
-    dk_ref[B:] = (dk_ref[B:].astype(jnp.float32) + dka[1] * scale).astype(jnp.bfloat16)
-    dv_ref[B:] = (dv_ref[B:].astype(jnp.float32) + dva[1]).astype(jnp.bfloat16)
-    out_k = pltpu.make_async_copy(dk_ref, dk_hbm, put.at[1])
-    out_v = pltpu.make_async_copy(dv_ref, dv_hbm, put.at[2])
-    out_k.start()
-    out_v.start()
-    for copy in (out_q, out_k, out_v):
+    give = Route(sems, 16, at.sibling, given_half, got_hbm)
+    give.start()
+    own_half[0] = (final[core, 0] + dka[0] * scale).astype(jnp.bfloat16)
+    own_half[1] = (final[core, 1] + dva[0]).astype(jnp.bfloat16)
+    out_own = pltpu.make_async_copy(own_half, own_hbm, put.at[1])
+    out_own.start()
+    give.arrived()
+    for copy in (out_q, out_own, out_rest):
         copy.wait()
     for copy in (
         far_back + side_up + side_down + bulk + back
-        + [far_up, far_down, near_up_0, near_up_1, near_down_0, near_down_1, give_k, give_v]
+        + [far_up, far_down, near_up_0, near_up_1, near_down_0, near_down_1, give]
     ):
         copy.sent()
 
@@ -772,11 +769,12 @@
         functools.partial(return_kernel, columns, heads),
         out_shape=(
             jax.ShapeDtypeStruct((rows, features), jnp.bfloat16),
-            jax.ShapeDtypeStruct((rows, W), jnp.bfloat16),
-            jax.ShapeDtypeStruct((rows, W), jnp.bfloat16),
+            jax.ShapeDtypeStruct(block, jnp.bfloat16),
+            jax.ShapeDtypeStruct(block, jnp.bfloat16),
+            jax.ShapeDtypeStruct(block, jnp.float32),
         ),
         in_specs=[vmem] + [some] * 9,
-        out_specs=(some,) * 3,
+        out_specs=(some,) * 4,
         scratch_shapes=[
             pltpu.VMEM(q.shape, q.dtype),
             pltpu.VMEM(k.shape, k.dtype),
@@ -787,8 +785,8 @@
             pltpu.VMEM(dq_own.shape, dq_own.dtype),
             pltpu.VMEM(dq_other.shape, dq_other.dtype),
             pltpu.VMEM(q.shape, jnp.bfloat16),
-            pltpu.VMEM((rows, W), jnp.bfloat16),
-            pltpu.VMEM((rows, W), jnp.bfloat16),
+            pltpu.VMEM(block, jnp.bfloat16),
+            pltpu.VMEM(block, jnp.float32),
             pltpu.VMEM((2, B, W), jnp.float32),
             pltpu.VMEM((2, B, W), jnp.float32),
             pltpu.VMEM((B, B), jnp.float32),
@@ -814,40 +812,52 @@
     )(docs, q, k, v, g, stat, dq_near, dq_own, dq_other, part)
 
 
-def publish_kernel(*refs):
-    sources, targets, held, get, put = refs[:3], refs[3:6], refs[6:9], refs[9], refs[10]
-    pieces = []
-    for source, target, mid in zip(sources, targets, held):
-        rows = min(source.shape[0], 128 * 1024 // source.shape[1])
-        for at in range(0, source.shape[0], rows):
-            here = slice(at, at + rows)
-            n = len(pieces)
-            pieces.append(
-                (
-                    pltpu.make_async_copy(source.at[here], mid.at[here], get.at[n]),
-                    pltpu.make_async_copy(mid.at[here], target.at[here], put.at[n]),
-                )
-            )
-    for into, _ in pieces:
-        into.start()
-    for into, out in pieces:
-        into.wait()
+def publish_kernel(
+    dq_ref, own_ref, got_ref, rest_ref, dq_out, dk_out, dv_out,
+    dq, own, got, rest, dk, dv, get, put,
+):
+    loads, outs = [], []
+    for n in range(4):
+        here = slice(n * B // 2, (n + 1) * B // 2)
+        loads.append(pltpu.make_async_copy(dq_ref.at[here], dq.at[here], get.at[n]))
+        outs.append(pltpu.make_async_copy(dq.at[here], dq_out.at[here], put.at[n]))
+    for n, (source, target) in enumerate(((own_ref, own), (got_ref, got), (rest_ref, rest))):
+        loads.append(pltpu.make_async_copy(source, target, get.at[4 + n]))
+    outs.append(pltpu.make_async_copy(dk, dk_out, put.at[4]))
+    outs.append(pltpu.make_async_copy(dv, dv_out, put.at[5]))
+    for copy in loads:
+        copy.start()
+    for load, out in zip(loads[:4], outs[:4]):
+        load.wait()
         out.start()
-    for _, out in pieces:
-        out.wait()
-
-
-def publish(*results):
+    for copy in loads[4:]:
+        copy.wait()
+    for n, target in enumerate((dk, dv)):
+        target[:B] = own[n]
+        target[B:] = (got[n].astype(jnp.float32) + rest[n]).astype(jnp.bfloat16)
+    for copy in outs[4:]:
+        copy.start()
+    for copy in outs:
+        copy.wait()
+
+
+def publish(dq, own, got, rest):
     some = pl.BlockSpec(memory_space=pl.ANY)
+    keys = (2 * B, W)
     return pl.pallas_call(
         publish_kernel,
-        out_shape=tuple(jax.ShapeDtypeStruct(x.shape, x.dtype) for x in results),
-        in_specs=[some] * 3,
+        out_shape=(
+            jax.ShapeDtypeStruct(dq.shape, dq.dtype),
+            jax.ShapeDtypeStruct(keys, jnp.bfloat16),
+            jax.ShapeDtypeStruct(keys, jnp.bfloat16),
+        ),
+        in_specs=[some] * 4,
         out_specs=(some,) * 3,
-        scratch_shapes=[pltpu.VMEM(x.shape, x.dtype) for x in results]
-        + [pltpu.SemaphoreType.DMA((6,))] * 2,
+        scratch_shapes=[pltpu.VMEM(x.shape, x.dtype) for x in (dq, own, got, rest)]
+        + [pltpu.VMEM(keys, jnp.bfloat16)] * 2
+        + [pltpu.SemaphoreType.DMA((7,)), pltpu.SemaphoreType.DMA((6,))],
         compiler_params=pltpu.CompilerParams(vmem_limit_bytes=VMEM),
-    )(*results)
+    )(dq, own, got, rest)
 
 
 def solution(mesh):
@@ -857,8 +867,7 @@
         docs = doc_lengths[None, :]
         q_other, g_other, stat, window, dq, sums = gather(columns, docs, q, g, o, k, v, log_total)
         dq_own, dq_other, part = attend(docs, q, q_other, g, g_other, stat, window, dq, sums)
-        dq, dk, dv = give_back(columns, docs, q, k, v, g, stat, dq, dq_own, dq_other, part)
-        return publish(dq, dk, dv)
+        return publish(*give_back(columns, docs, q, k, v, g, stat, dq, dq_own, dq_other, part))
 
     rows = P(("ctx", "section"), None)
     return jax.shard_map(

time: 77 us -> 78.1 us (1.014)
  the two profiles are of different devices: /device:TPU:11 before, /device:TPU:5 now
where the time goes in v4:
time: 78.1 us; the launch traced here: 77.9 us
  Pallas kernels  77.1 us (99%)
  between operations  0.81 us (1%)
    pallas_call x1, Pallas kernels, gather(): pl.pallas_call(functools.partial(gather_kernel, columns, heads), out_shap...  27.6 us
    pallas_call x1, Pallas kernels, attend(): pl.pallas_call(functools.partial(attend_kernel, heads), out_shape=(jax.Sh...  24.5 us
    pallas_call x1, Pallas kernels, give_back(): pl.pallas_call(functools.partial(return_kernel, columns, heads), out_shap...  22.8 us
    pallas_call x1, Pallas kernels, publish(): pl.pallas_call(publish_kernel, out_shape=(jax.ShapeDtypeStruct(dq.shape,...  2.18 us

profile of v4, /device:TPU:5, one launch (start us, length us, event | category | flops | bytes accessed | tf_op | source)
XLA Modules:
  0.0 77.9 jit_solution(13965213325940759017)
XLA Ops:
  0.6 27.6 %shard_map.94 = (bf16[512,1024]{1,0:T(8,128)(2,1)}, bf16[512,1024]{1,0:T(8,128)(2,1)}, f32[2,2,8,512]{3,2,1,0:T(8,128)}, bf16[16,2,256,128]{3,2,1,0:T(8,128)(2,1...) custom-call(s32[1,128]{1,0:T(1,128)} %bitcast.1, bf16[512,1024]{1,0:T(8,128)(2,1)} %q_hbm.1, ...), custom_call_target="tpu_custom_call" | custom-call | tf_op jit(solution)/shard_map/pallas_call | solution.py:356
  28.2 24.5 %shard_map.95 = (f32[2,128,2048]{2,1,0:T(8,128)}, bf16[2,128,2048]{2,1,0:T(8,128)(2,1)}, bf16[16,2,256,128]{3,2,1,0:T(8,128)(2,1)}) custom-call(s32[1,128]{1,0:T(1,128)} %bitcast.2, bf16[512,1024]{1,0:T(8,128)(2,1)} %q_hbm.1, bf16[512,1024]{1,0:T(8,128)(2,1)} %get-tuple-element.18.qb_hbm, bf16[512,1024]{1,0:T(8,128)(2,1)} %g_hbm.1, ...), custom_call_target="tpu_custom_call" | custom-call | flops 13421772800 | bytes 16777216 | tf_op jit(solution)/shard_map/pallas_call | solution.py:533
  52.8 22.8 %shard_map.96 = (bf16[512,1024]{1,0:T(8,128)(2,1)}, bf16[2,256,128]{2,1,0:T(8,128)(2,1)}, bf16[2,256,128]{2,1,0:T(8,128)(2,1)}, f32[2,256,128]{2,1,0:T(8,128)}) custom-call(s32[1,128]{1,0:T(1,128)} %bitcast.3, bf16[512,1024]{1,0:T(8,128)(2,1)} %q_hbm.1, bf16[512,128]{1,0:T(8,128)(2,1)} %k_hbm.1, bf16[512,128]{1,0:T(8,128)(2,1)} %v_hbm.1, ...), custom_call_target="tpu_custom_call" | custom-call | tf_op jit(solution)/shard_map/pallas_call | solution.py:768
  75.6 2.2 %shard_map.97 = (bf16[512,1024]{1,0:T(8,128)(2,1)}, bf16[512,128]{1,0:T(8,128)(2,1)}, bf16[512,128]{1,0:T(8,128)(2,1)}) custom-call(bf16[512,1024]{1,0:T(8,128)(2,1)} %get-tuple-element.25.dq_ref, bf16[2,256,128]{2,1,0:T(8,128)(2,1)} %get-tuple-element.26.own_ref, bf16[2,256,128]{2,1,0:T(8,128)(2,1)} %get-tuple-element.27.got_ref, ...), custom_call_target="tpu_custom_call" | custom-call | tf_op jit(solution)/shard_map/pallas_call | solution.py:847
